TPU v7x, 512 devices: a whole 4x8x8 slice. The times are simulated.
512 devices in a mesh: af: 64 (over z, x, core), gx: 8 (over y).
Axes of the slice: x: 4, y: 8, z: 8, core: 2. Of those that a mesh axis runs over, the one named last changes fastest.
Arguments:
- volts: bfloat16 [1024, 128, 2, 1024], P('af', 'gx'), may hold values from -6 to 6
- history: bfloat16 [1024, 128, 2, 1408], P('af', 'gx'), may hold values from -6 to 6
- pfb_taps: float32 [12, 128], replicated, may hold values from -1.75 to 1.75
- zoom_bins: int32 [16384, 1], replicated, may hold values from 0 to 63, as said below
- counts: int32 [16384], replicated, may hold values from 1 to 8
- beam_stations: int32 [6, 256], replicated, may hold values from 0 to 511
- beam_weights: float32 [2, 6, 1024], replicated, may hold values from -0.125 to 0.125
Outputs:
- vis: bfloat16 [64, 8, 1024, 1024], P('af', 'gx')
- beam_power: float32 [6, 128, 128, 8], P(None, 'gx', 'af')
Inputs may be any that keep to these rules, and one draw needn't show every extreme that they name: `zoom_bins`: within each aligned block of 2048 entries (one channel group) no bin is named by more than 64 channels; in every block one bin is named by exactly 64 channels and at least one bin by none. `beam_stations`: entries may repeat; a repeated station counts once for each entry.
All inputs are finite; a program needn't handle non-finite values.
Results may differ from a plain program's by a relative error of at most 0.0079.
Values may be sent and summed in bfloat16 or wider, within the bound.
A program may use at most 128 MiB of HBM per device.

v0:
```python
import jax
import jax.numpy as jnp
from jax import lax
from jax.sharding import PartitionSpec as P


def dft_table(fine):
    index = jnp.arange(fine, dtype=jnp.int32)
    product = index[:, None] * index[None, :] % fine
    angle = product.astype(jnp.float32) * jnp.float32(2.0 * 3.141592653589793 / fine)
    cosine = jnp.cos(angle) / jnp.sqrt(jnp.float32(fine))
    sine = jnp.sin(angle) / jnp.sqrt(jnp.float32(fine))
    first_row = jnp.stack([cosine, -sine], 1)
    second_row = jnp.stack([sine, cosine], 1)
    return jnp.stack([first_row, second_row], 0).astype(jnp.bfloat16)


def channelize(extended, filter_taps, table):
    inputs_here, coarse, parts, length = extended.shape
    fine = filter_taps.shape[1]
    tap_count = filter_taps.shape[0]
    frames = extended.reshape(inputs_here, coarse, parts, length // fine, fine)
    steps = length // fine - tap_count + 1
    filtered = frames[:, :, :, 0:steps, :] * filter_taps[0]
    for offset in range(1, tap_count):
        filtered = filtered + frames[:, :, :, offset : offset + steps, :] * filter_taps[offset]
    filtered = filtered.astype(jnp.bfloat16)
    result = jnp.einsum("icrtn,rnsk->istck", filtered, table, preferred_element_type=jnp.float32)
    return result.astype(jnp.bfloat16)


def beam_matrix(station_lists, weights, first_input, input_count):
    station_ids = (first_input + jnp.arange(input_count, dtype=jnp.int32)) // 2
    member = jnp.sum(
        (station_lists[:, :, None] == station_ids[None, None, :]).astype(jnp.float32), axis=1
    )
    chosen = lax.dynamic_slice_in_dim(weights, first_input, input_count, 2)
    weight_re = (member * chosen[0]).T
    weight_im = (member * chosen[1]).T
    inner_first = jnp.stack([weight_re, weight_im], -1)
    inner_second = jnp.stack([-weight_im, weight_re], -1)
    return jnp.stack([inner_first, inner_second], 1).astype(jnp.bfloat16)


def slot_table(bins_group, bin_count, capacity):
    size = bins_group.shape[0]
    bin_ids = jnp.arange(bin_count, dtype=jnp.int32)
    hits = (bins_group[:, None] == bin_ids[None, :]).astype(jnp.int32)
    per_bin = jnp.sum(hits, axis=0)
    starts = jnp.cumsum(per_bin) - per_bin
    order = jnp.argsort(bins_group, stable=True)
    sorted_bins = jnp.take(bins_group, order)
    first = jnp.sum(jnp.where(sorted_bins[:, None] == bin_ids[None, :], starts[None, :], 0), axis=1)
    rank = jnp.arange(size, dtype=jnp.int32) - first
    target = sorted_bins * capacity + rank
    source = jnp.zeros((bin_count * capacity,), jnp.int32).at[target].set(order)
    filled = (
        jnp.zeros((bin_count * capacity,), jnp.int32).at[target].set(jnp.ones((size,), jnp.int32))
    )
    return (source.reshape(bin_count, capacity), filled.reshape(bin_count, capacity))


def per_device(volts, history, pfb_taps, zoom_bins, counts, beam_stations, beam_weights):
    bin_index = lax.axis_index("af")
    group_index = lax.axis_index("gx")
    bin_count = lax.axis_size("af")
    local_inputs = volts.shape[0]
    fine = pfb_taps.shape[1]
    extended = jnp.concatenate([history, volts], axis=3)
    spectra = channelize(extended, pfb_taps, dft_table(fine))
    local_steps = spectra.shape[2]
    all_inputs = local_inputs * bin_count
    weights_eff = beam_matrix(beam_stations, beam_weights, bin_index * local_inputs, local_inputs)
    partial_beams = jnp.einsum(
        "irtck,irbs->bsckt", spectra, weights_eff, preferred_element_type=jnp.float32
    )
    beams = lax.psum_scatter(partial_beams, "af", scatter_dimension=3, tiled=True)
    beam_power = beams[:, 0] * beams[:, 0] + beams[:, 1] * beams[:, 1]
    group_local = lax.all_to_all(spectra, "gx", split_axis=4, concat_axis=3, tiled=True)
    group_size = group_local.shape[3] * group_local.shape[4]
    flat_group = group_local.reshape(local_inputs, 2, local_steps, group_size)
    capacity = 2 * group_size // bin_count
    start = group_index * group_size
    bins_group = lax.dynamic_slice_in_dim(zoom_bins[:, 0], start, group_size)
    counts_group = lax.dynamic_slice_in_dim(counts, start, group_size)
    source, filled = slot_table(bins_group, bin_count, capacity)
    slots = jnp.take(flat_group, source.reshape(-1), axis=3).reshape(
        local_inputs, 2, local_steps, bin_count, capacity
    )
    received = lax.all_to_all(slots, "af", split_axis=3, concat_axis=0, tiled=True)
    received = received.reshape(all_inputs, 2, local_steps, capacity)
    row_source = lax.dynamic_index_in_dim(source, bin_index, 0, keepdims=False)
    row_filled = lax.dynamic_index_in_dim(filled, bin_index, 0, keepdims=False)
    slot_counts = jnp.where(row_filled == 1, jnp.take(counts_group, row_source), 0)
    time_ids = jnp.arange(local_steps, dtype=jnp.int32)
    valid = time_ids[:, None] < slot_counts[None, :]
    masked = jnp.where(valid[None, None], received, jnp.zeros((), jnp.bfloat16))
    flat = masked.reshape(all_inputs, 2 * local_steps * capacity)
    contract = (((1,), (1,)), ((), ()))
    real_part = lax.dot_general(flat, flat, contract, preferred_element_type=jnp.float32)
    part_re = masked[:, 0].reshape(all_inputs, local_steps * capacity)
    part_im = masked[:, 1].reshape(all_inputs, local_steps * capacity)
    cross = lax.dot_general(part_im, part_re, contract, preferred_element_type=jnp.float32)
    imag_part = cross - cross.T
    total = jnp.sum(jnp.where(bins_group == bin_index, counts_group, 0))
    row_ids = jnp.arange(all_inputs, dtype=jnp.int32)
    upper = row_ids[None, :] >= row_ids[:, None]
    scale = jnp.maximum(total, 1).astype(jnp.float32)
    vis = (jnp.where(upper, real_part, imag_part) / scale).astype(jnp.bfloat16)
    return (vis[None, None], beam_power)


def solution(mesh):
    in_specs = (P("af", "gx", None, None), P("af", "gx", None, None), P(), P(), P(), P(), P())
    out_specs = (P("af", "gx", None, None), P(None, "gx", "af", None))
    return jax.shard_map(
        per_device, mesh=mesh, in_specs=in_specs, out_specs=out_specs, check_vma=False
    )
```

profile of v0, /device:TPU:1, one launch (start us, length us, event | category | flops | bytes accessed | tf_op | source)
XLA Modules:
  0.0 392.6 jit_solution(7013837239605903644)
XLA Ops:
  7.2 0.3 fusion.22
  7.4 0.3 negate_convert_fusion
  7.7 1.0 slice_bitcast_fusion.15
  8.7 3.9 %pad_maximum_fusion = bf16[16,16,2,2432]{3,2,1,0:T(2,128)(2,1)S(1)} fusion(bf16[16,16,2,1024]{3,2,1,0:T(2,128)(2,1)} %param.7, bf16[16,16,2,1408]{3,2,1,0:T(2,128)(2,1)} %param.8), kind=kLoop, calls=%fused_computation.14 | loop fusion | flops 4980736 | bytes 4980736 | tf_op jit(solution)/shard_map/concatenate | solution.py:69
  12.7 1.7 copy.62
  14.4 4.1 %reshape.264 = bf16[16,16,2,19,128]{4,3,1,2,0:T(8,128)(2,1)S(1)} reshape(bf16[16,16,2,2432]{3,1,2,0:T(8,128)(2,1)} %copy.62) | data formatting | bytes 4980736 | tf_op jit(solution)/shard_map/reshape | solution.py:22
  18.4 3.4 add_convert_fusion
  21.8 0.4 fusion.9
  22.3 11.8 %copy.64 = bf16[16,2,8,16,128]{3,2,0,1,4:T(8,128)(2,1)} copy(bf16[16,2,8,16,128]{4,3,2,0,1:T(8,128)(2,1)S(1)} %fusion.9) | data formatting | bytes 2097152 | tf_op jit(solution)/shard_map/convert_element_type | solution.py:29
  34.1 11.2 %reshape.327 = bf16[8,2,32768]{2,1,0:T(2,128)(2,1)} reshape(bf16[128,2,16,8,16]{4,3,2,1,0:T(8,128)(2,1)} %bitcast.167) | data formatting | bytes 2097152
  45.4 7.7 %all-to-all-start = ((bf16[8,2,32768]{2,1,0:T(2,128)(2,1)}), bf16[8,2,32768]{2,1,0:T(2,128)(2,1)S(1)}, u32[]{:S(2)}, u32[]{:S(2)}) async-start(bf16[8,2,32768]{2,1,0:T(2,128)(2,1)} %reshape.327), calls=%async_computation | async-start | bytes 2097152 | tf_op jit(solution)/shard_map/all_to_all | solution.py:79
  53.1 5.0 %sort.17 = (s32[2048]{0:T(1024)}, s32[2048]{0:T(1024)S(1)}) sort(s32[2048]{0:T(1024)S(1)} %bitcast.162, s32[2048]{0:T(1024)S(1)} %iota.55), dimensions={0}, to_apply=%region_0.1 | sort | flops 22528 | bytes 32768 | tf_op jit(solution)/shard_map/jit(argsort)/sort | solution.py:51
  58.1 11.8 %gather_fusion = s32[2048]{0:T(1024)S(1)} fusion(s32[2048]{0:T(1024)S(1)} %bitcast.163, s32[2048]{0:T(1024)S(1)} %fusion.32), kind=kCustom, calls=%fused_computation | custom fusion | bytes 24576 | tf_op jit(solution)/shard_map/jit(_take)/gather | solution.py:52
  69.9 0.2 convert_reduce_fusion
  70.0 0.1 copy.60
  70.1 0.1 reduce-window.8
  70.2 0.1 reduce
  70.4 0.2 select_reduce_fusion
  70.6 8.2 %scatter_custom_fusion.1 = s32[4096]{0:T(1024)S(1)} fusion(s32[2048]{0:T(1024)S(1)} %compare_select_fusion.1, s32[2048]{0:T(1024)S(1)} %get-tuple-element.3, s32[]{:T(128)} %constant.66.clone.1), kind=kCustom, calls=%fused_computation.64 | custom fusion | bytes 16388 | tf_op jit(solution)/shard_map/scatter | solution.py:56
  78.8 0.1 broadcast_in_dim.89
  78.9 1.3 all-to-all-done
  80.2 7.5 %reshape.328 = bf16[128,2,16,8,16]{4,3,2,1,0:T(8,128)(2,1)} reshape(bf16[8,2,32768]{2,1,0:T(2,128)(2,1)S(1)} %all-to-all-done) | data formatting | bytes 2097152
  87.7 18.7 %copy.82 = bf16[16,2,8,8,16,16]{0,2,5,4,3,1:T(8,128)(2,1)} copy(bf16[16,2,8,8,16,16]{4,2,0,1,5,3:T(8,128)(2,1)} %bitcast.168) | data formatting | bytes 2097152 | tf_op jit(solution)/shard_map/reshape | solution.py:81
  106.5 35.9 %gather_fusion.2 = bf16[4096,16,2,8]{1,3,2,0:T(8,128)(2,1)} fusion(bf16[16,2,8,2048]{0,2,3,1:T(8,128)(2,1)} %bitcast.171, s32[4096]{0:T(1024)S(1)} %fusion.25), kind=kCustom, calls=%fused_computation.2 | custom fusion | bytes 4210688 | tf_op jit(solution)/shard_map/jit(_take)/gather | solution.py:87
  142.4 19.9 %copy.83 = bf16[16,2,8,64,64]{4,3,2,1,0:T(8,128)(2,1)} copy(bf16[16,2,8,64,64]{0,2,1,4,3:T(8,128)(2,1)} %bitcast.169) | data formatting | bytes 4194304 | tf_op jit(solution)/shard_map/jit(_take)/gather | solution.py:87
  162.3 2.5 broadcast_select_fusion
  164.8 4.6 %copy.121 = bf16[16,2,8,64,64]{4,2,1,0,3:T(8,128)(2,1)} copy(bf16[16,2,8,64,64]{4,3,2,1,0:T(8,128)(2,1)S(1)} %broadcast_select_fusion) | data formatting | bytes 4194304 | tf_op jit(solution)/shard_map/jit(_take)/select_n | solution.py:87
  169.4 7.9 %reshape.329 = bf16[64,2,8192]{2,1,0:T(2,128)(2,1)} reshape(bf16[64,16,2,8,64]{4,3,2,1,0:T(8,128)(2,1)} %bitcast.170) | data formatting | bytes 4194304
  177.3 16.0 %all-to-all-start.1 = ((bf16[64,2,8192]{2,1,0:T(2,128)(2,1)}), bf16[64,2,8192]{2,1,0:T(2,128)(2,1)S(1)}, u32[]{:S(2)}, u32[]{:S(2)}) async-start(bf16[64,2,8192]{2,1,0:T(2,128)(2,1)} %reshape.329), calls=%async_computation.1 | async-start | bytes 4194304 | tf_op jit(solution)/shard_map/all_to_all | solution.py:90
  193.4 0.9 constant_dynamic-slice_fusion.1
  194.2 0.2 convert_reduce_fusion.1
  194.4 1.7 convolution_bitcast_fusion.1
  196.2 4.9 %copy.75 = f32[6,2,16,128,8]{2,4,1,0,3:T(8,128)} copy(f32[6,2,16,128,8]{3,0,2,4,1:T(8,128)} %convolution_bitcast_fusion.1) | data formatting | bytes 1572864 | tf_op jit(solution)/shard_map/irtck,irbs->bsckt/transpose | solution.py:74
  201.1 0.1 reshape.263
  201.1 1.3 select_reduce_fusion.1
  203.1 8.3 %scatter_custom_fusion = s32[4096]{0:T(1024)S(1)} fusion(s32[2048]{0:T(1024)S(1)} %compare_select_fusion.1, s32[2048]{0:T(1024)S(1)} %broadcast.249, s32[]{:T(128)} %constant.66.clone.1), kind=kCustom, calls=%fused_computation.66 | custom fusion | bytes 16388 | tf_op jit(solution)/shard_map/scatter | solution.py:58
  211.4 0.1 reshape.262
  211.5 0.8 gather_fusion.1
  212.3 138.4 %reduce-scatter.2.cloned.1.call-done = f32[6,2,16,2,8]{2,4,1,0,3:T(8,128)} async-done(((f32[6,2,16,128,8]{2,4,1,0,3:T(8,128)}), f32[6,2,16,2,8]{2,4,1,0,3:T(8,128)}) %reduce-scatter.2.cloned.1.call-update) | async-done | bytes 12304 | tf_op jit(solution)/shard_map/reduce_scatter | solution.py:77
  350.7 0.8 fusion.24
  351.5 0.6 copy.76
  352.1 4.0 %reshape.330 = bf16[64,16,2,8,64]{4,3,2,1,0:T(8,128)(2,1)} reshape(bf16[64,2,8192]{2,1,0:T(2,128)(2,1)S(1)} %all-to-all-done.1) | data formatting | bytes 4194304
  356.2 4.5 %copy.71 = bf16[1024,2,8,64]{0,3,2,1:T(8,128)(2,1)S(1)} copy(bf16[1024,2,8,64]{3,2,1,0:T(8,128)(2,1)} %bitcast.166) | data formatting | bytes 4194304 | tf_op jit(solution)/shard_map/reshape | solution.py:91
  360.7 4.4 %bitcast_select_fusion.1 = bf16[64,16,2,8,1,64]{5,3,2,1,0,4:T(8,128)(2,1)} fusion(pred[8,64]{1,0:T(8,128)(4,1)S(1)} %iota_compare_fusion.3, bf16[64,16,2,8,64]{4,3,2,1,0:T(8,128)(2,1)} %reshape.330), kind=kLoop, calls=%fused_computation.9 | loop fusion | flops 1048576 | bytes 4194816 | tf_op jit(solution)/shard_map/jit(_where)/select_n | solution.py:97
  365.1 0.2 broadcast_select_fusion.1
  365.3 3.2 convolution_bitcast_fusion
  368.5 5.3 %copy.72 = f32[1024,1024]{0,1:T(8,128)} copy(f32[1024,1024]{1,0:T(8,128)} %convolution_bitcast_fusion) | data formatting | bytes 8388608 | tf_op jit(solution)/shard_map/dot_general | solution.py:103
  373.9 11.9 %fusion.6 = bf16[1,1,1024,1024]{3,2,1,0:T(8,128)(2,1)} fusion(f32[]{:T(128)S(6)} %convert_element_type.100, f32[1024,1024]{1,0:T(8,128)} %convolution_bitcast_fusion, f32[1024,1024]{0,1:T(8,128)} %copy.72, bf16[1024,2,8,64]{3,2,1,0:T(8,128)(2,1)} %bitcast.172), kind=kOutput, calls=%fused_computation.19 | convolution fusion | flops 2152726528 | bytes 12582916 | tf_op jit(solution)/shard_map/dot_general | solution.py:100
  (26 shorter events, 0.2 us)
Async XLA Ops:
  7.2 45.9 %copy-start = (s32[16384,1]{0,1:T(1,128)S(1)}, s32[16384,1]{0,1:T(1,128)}, u32[]{:S(2)}) copy-start(s32[16384,1]{0,1:T(1,128)} %param.10) | copy-start | bytes 196612
  45.4 34.8 %all-to-all-start = ((bf16[8,2,32768]{2,1,0:T(2,128)(2,1)}), bf16[8,2,32768]{2,1,0:T(2,128)(2,1)S(1)}, u32[]{:S(2)}, u32[]{:S(2)}) async-start(bf16[8,2,32768]{2,1,0:T(2,128)(2,1)} %reshape.327), calls=%async_computation | async-start | bytes 2097152 | tf_op jit(solution)/shard_map/all_to_all | solution.py:79
  177.3 16.9 %copy-start.2 = (s32[6,256]{1,0:T(8,128)S(1)}, s32[6,256]{1,0:T(8,128)}, u32[]{:S(2)}) copy-start(s32[6,256]{1,0:T(8,128)} %param.12) | copy-start | bytes 18436
  177.3 174.8 %all-to-all-start.1 = ((bf16[64,2,8192]{2,1,0:T(2,128)(2,1)}), bf16[64,2,8192]{2,1,0:T(2,128)(2,1)S(1)}, u32[]{:S(2)}, u32[]{:S(2)}) async-start(bf16[64,2,8192]{2,1,0:T(2,128)(2,1)} %reshape.329), calls=%async_computation.1 | async-start | bytes 4194304 | tf_op jit(solution)/shard_map/all_to_all | solution.py:90
  193.3 157.4 %reduce-scatter.2.cloned.1.call-start = ((), (), s32[]{:S(2)}) async-start(), calls=%async_computation.3 | async-start | bytes 6389760 | tf_op jit(solution)/shard_map/reduce_scatter | solution.py:77
  373.9 11.9 %copy-start.1 = (s32[16384,1]{0,1:T(1,128)S(1)}, s32[16384,1]{0,1:T(1,128)}, u32[]{:S(2)}) copy-start(s32[16384,1]{0,1:T(1,128)} %param.10) | copy-start | bytes 196612
Sparse Core Ops, SparseCore 0:
  201.2 149.4 reduce-scatter.1
where the time goes:
time: 399 us; the launch traced here: 393 us
  local copies, waits for them, and re-layouts  174 us (44%)
  waiting for transfers between devices  140 us (35%)
  starting transfers between devices  23.7 us (6%)
  other arithmetic  23 us (6%)
  matrix products  17.3 us (4%)
  between operations  14.9 us (4%)
    reduce_scatter x1, waiting for transfers between devices, per_device(): lax.psum_scatter(partial_beams, 'af', scatter_dimension=3, tiled=True)  138 us
    gather x2, local copies, waits for them, and re-layouts, per_device(): jnp.take(flat_group, source.reshape(-1), axis=3)  55.8 us
    unnamed x11, local copies, waits for them, and re-layouts  31.3 us
    reshape x1, local copies, waits for them, and re-layouts, per_device(): flat_group = group_local.reshape(local_inputs, 2, local_steps, group_size)  18.7 us
    all_to_all x1, starting transfers between devices, per_device(): lax.all_to_all(slots, 'af', split_axis=3, concat_axis=0, tiled=True)  16 us
    dot_general x1, matrix products, per_device(): lax.dot_general(flat, flat, contract, preferred_element_type=jnp.float32)  11.9 us
    convert_element_type x1, local copies, waits for them, and re-layouts, channelize(): return result.astype(jnp.bfloat16)  11.8 us
    gather x1, local copies, waits for them, and re-layouts, slot_table(): sorted_bins = jnp.take(bins_group, order)  11.8 us
  transfers between devices with their start and end apart: 3, of which 2 were waited for; matrix products, arithmetic and copies ran while one was open for 12% of the time, Pallas kernels for 0%

commit v1 on v0

v1 whole, which is shorter than its diff:
```python
import jax
import jax.numpy as jnp
import numpy as np
from jax import lax
from jax.experimental import pallas as pl
from jax.experimental.pallas import tpu as pltpu
from jax.sharding import PartitionSpec as P

FINE = 128
TAPS = 12
NT = 8
NB = 6
BINS = 64
GROUPS = 8
LOCAL = 16
COARSE = 16
CHG = 2048
NIN = 1024
HALF = 4
LANES = 512
MESH = pl.DeviceIdType.MESH
CONTRACT_LANES = (((1,), (1,)), ((), ()))
CONTRACT_ROWS = (((0,), (0,)), ((), ()))


def dft_rows():
    index = np.arange(FINE)
    angle = (index[:, None] * index[None, :] % FINE) * (2.0 * np.pi / FINE)
    cosine = np.cos(angle) / np.sqrt(FINE)
    sine = np.sin(angle) / np.sqrt(FINE)
    return jnp.asarray(np.concatenate([cosine.T, sine.T], axis=1), jnp.bfloat16)


def to(device):
    return dict(device_id=device, device_id_type=MESH)


def kernel(
    volts, history, aux, table, taps, weights,
    vis, power,
    frames, filt, ysend, yrecv, pick, outgo, arrived, acc, visbuf,
    beams, bsend0, brecv0, bsend1, brecv1, bsend2, brecv2,
    frame_sem, ysend_sem, yrecv_sem, send_sem, recv_sem,
    bsend_sem, brecv_sem, vis_sem,
):
    me = lax.axis_index("af")
    gx = lax.axis_index("gx")
    my_z = me // 8
    my_x = (me // 2) % 4
    my_core = me % 2
    my_low = me % 8
    f32, bf16 = jnp.float32, jnp.bfloat16

    barrier = pltpu.get_barrier_semaphore()

    def greet(d, carry):
        pl.semaphore_signal(barrier, inc=1, **to({"af": (me + d) % BINS}))
        return carry

    lax.fori_loop(1, BINS, greet, 0)

    def greet_gx(d, carry):
        pl.semaphore_signal(barrier, inc=1, **to({"gx": (gx + d) % GROUPS}))
        return carry

    lax.fori_loop(1, GROUPS, greet_gx, 0)

    def fetch(i, carry):
        def old(f, c):
            cut = pl.ds(pl.multiple_of(f * FINE, FINE), FINE)
            pltpu.make_async_copy(history.at[i, :, :, cut], frames.at[:, f, i], frame_sem).start()
            return c

        lax.fori_loop(0, TAPS - 1, old, 0)

        def new(f, c):
            cut = pl.ds(pl.multiple_of(f * FINE, FINE), FINE)
            pltpu.make_async_copy(volts.at[i, :, :, cut], frames.at[:, TAPS - 1 + f, i], frame_sem).start()
            return c

        lax.fori_loop(0, NT, new, 0)
        return carry

    lax.fori_loop(0, LOCAL, fetch, 0)
    pltpu.make_async_copy(frames, frames, frame_sem).wait()

    frame_rows = frames.reshape(COARSE, NT + TAPS - 1, 2 * LOCAL, FINE)

    def channelize(half):
        def one(c, carry):
            for t in range(HALF):
                first = half * HALF + t
                total = frame_rows[c, first].astype(f32) * taps[0:1, :]
                for j in range(1, TAPS):
                    total = total + frame_rows[c, first + j].astype(f32) * taps[j : j + 1, :]
                filt[pl.ds(t * 2 * LOCAL, 2 * LOCAL), :] = total
            re = filt[pl.ds(0, HALF * LOCAL, stride=2), :].astype(bf16)
            im = filt[pl.ds(1, HALF * LOCAL, stride=2), :].astype(bf16)
            rows = jnp.concatenate(
                [jnp.concatenate([re, im], axis=1), jnp.concatenate([im, -re], axis=1)], axis=0
            )
            spectra = lax.dot_general(
                table[...], rows, CONTRACT_LANES, preferred_element_type=f32
            ).astype(bf16)
            ysend[half, :, c] = spectra.reshape(GROUPS, 16, FINE)
            part = jnp.dot(spectra, weights[half], preferred_element_type=f32)
            spot = pl.ds(c, FINE, stride=COARSE)
            if half == 0:
                beams[spot, :] = part
            else:
                beams[spot, :] = beams[spot, :] + part
            return carry

        lax.fori_loop(0, COARSE, one, 0)

    def send_spectra(half):
        def one(d, carry):
            dest = (gx + d) % GROUPS
            pltpu.make_async_remote_copy(
                src_ref=ysend.at[half, dest],
                dst_ref=yrecv.at[half, gx],
                send_sem=ysend_sem.at[half],
                recv_sem=yrecv_sem.at[half],
                **to({"gx": dest}),
            ).start()
            return carry

        lax.fori_loop(1, GROUPS, one, 0)
        yrecv[half, gx] = ysend[half, gx]

    channelize(0)
    pl.semaphore_wait(barrier, BINS - 1 + GROUPS - 1)
    send_spectra(0)
    channelize(1)
    send_spectra(1)

    def pack0(s, carry):
        row = pl.multiple_of((s * 2 + 1 - my_core) * 32, 32)
        bsend0[s] = beams[pl.ds(row, 32), :].astype(bf16)
        return carry

    lax.fori_loop(0, 32, pack0, 0)
    sibling = my_z * 8 + my_x * 2 + 1 - my_core
    core_copy = pltpu.make_async_remote_copy(
        src_ref=bsend0, dst_ref=brecv0, send_sem=bsend_sem.at[0], recv_sem=brecv_sem.at[0],
        **to({"af": sibling}),
    )
    core_copy.start()

    lane = lax.broadcasted_iota(jnp.int32, (256, FINE), 1)
    lower = (
        lax.broadcasted_iota(jnp.int32, (256, 256), 1) < lax.broadcasted_iota(jnp.int32, (256, 256), 0)
    ).astype(f32).astype(bf16)

    def place(block, seen):
        rows = pl.ds(pl.multiple_of(block * 256, 256), 256)
        hits = jnp.where(lane < BINS, aux[rows, :].astype(f32), 0.0)
        before = jnp.dot(lower, hits.astype(bf16), preferred_element_type=f32) + seen
        target = jnp.sum(hits * (before + (lane * 64).astype(f32)), axis=1, keepdims=True)
        target = jnp.broadcast_to(target, (256, FINE)).astype(jnp.int32)

        def column(z, carry):
            for p in range(4):
                here = lane + (z * 512 + p * FINE)
                pick[z, rows, p * FINE : (p + 1) * FINE] = (target == here).astype(f32).astype(bf16)
            return carry

        lax.fori_loop(0, 8, column, 0)
        return seen + jnp.sum(hits, axis=0, keepdims=True)

    lax.fori_loop(0, CHG // 256, place, jnp.zeros((1, FINE), f32))

    tally = lax.dot_general(aux[...], aux[...], CONTRACT_ROWS, preferred_element_type=f32)
    row_id = lax.broadcasted_iota(jnp.int32, (FINE, FINE), 0)
    col_id = lax.broadcasted_iota(jnp.int32, (FINE, FINE), 1)
    mine = jnp.logical_and(row_id == me, jnp.logical_and(col_id >= 64, col_id < 64 + NT))
    count = jnp.sum(jnp.where(mine, tally, 0.0), axis=1, keepdims=True)
    count = jnp.sum(count, axis=0, keepdims=True)
    scale = 1.0 / jnp.maximum(count, 1.0)

    def distribute(half):
        pltpu.make_async_copy(
            yrecv.at[half, pl.ds(0, GROUPS - 1)], yrecv.at[half, pl.ds(0, GROUPS - 1)], yrecv_sem.at[half]
        ).wait()
        spread = (row_id == 64 + half * HALF + (col_id // LOCAL) % HALF).astype(f32).astype(bf16)
        valid = jnp.dot(aux[...], spread, preferred_element_type=f32)
        samples = yrecv[half].reshape(CHG, FINE).astype(f32)
        flipped = jnp.where(valid > 0.5, samples, 0.0).T.astype(bf16)
        low = lax.broadcasted_iota(jnp.int32, (LOCAL, FINE), 1) < 64

        def one(step, carry):
            turn = 7 - step
            hop = ((turn + 1) // 2) * (2 * (turn % 2) - 1)
            z = (my_z + hop + 8) % 8
            picked = jnp.dot(flipped, pick[z], preferred_element_type=f32)
            for pair in range(4):
                for s in range(2):
                    for tp in range(2):
                        row = s * 64 + tp * 32
                        first = picked[row : row + 16, pair * FINE : (pair + 1) * FINE]
                        second = picked[row + 16 : row + 32, pair * FINE : (pair + 1) * FINE]
                        second = pltpu.roll(second, 64, 1)
                        cols = slice((s * 2 + tp) * FINE, (s * 2 + tp + 1) * FINE)
                        outgo[half, z * 8 + 2 * pair, :, cols] = jnp.where(low, first, second).astype(bf16)
                        outgo[half, z * 8 + 2 * pair + 1, :, cols] = jnp.where(low, second, first).astype(bf16)

            def send(k, c):
                dest = z * 8 + (my_low + k) % 8

                @pl.when(dest != me)
                def _():
                    pltpu.make_async_remote_copy(
                        src_ref=outgo.at[half, dest],
                        dst_ref=arrived.at[half, pl.ds(pl.multiple_of(me * LOCAL, LOCAL), LOCAL)],
                        send_sem=send_sem.at[half],
                        recv_sem=recv_sem.at[half],
                        **to({"af": dest}),
                    ).start()

                return c

            lax.fori_loop(0, 8, send, 0)
            return carry

        lax.fori_loop(0, 8, one, 0)
        arrived[half, pl.ds(pl.multiple_of(me * LOCAL, LOCAL), LOCAL)] = outgo[half, me]

    def correlate(half):
        others = pl.ds(0, (BINS - 1) * LOCAL)
        pltpu.make_async_copy(arrived.at[half, others], arrived.at[half, others], recv_sem.at[half]).wait()

        def stripe(bi, carry):
            rows = pl.ds(pl.multiple_of(bi * 256, 256), 256)
            left = arrived[half, rows, :]
            turned = jnp.concatenate([left[:, 256:], -left[:, :256]], axis=1)

            def block(bj, c):
                cols = pl.ds(pl.multiple_of(bj * 256, 256), 256)
                right = arrived[half, cols, :]

                def finish(value):
                    if half == 0:
                        acc[bi, bj] = value
                    else:
                        visbuf[rows, cols] = ((acc[bi, bj] + value) * scale).astype(bf16)

                @pl.when(bj > bi)
                def _():
                    finish(lax.dot_general(left, right, CONTRACT_LANES, preferred_element_type=f32))

                @pl.when(bj < bi)
                def _():
                    finish(lax.dot_general(turned, right, CONTRACT_LANES, preferred_element_type=f32))

                @pl.when(bj == bi)
                def _():
                    real = lax.dot_general(left, right, CONTRACT_LANES, preferred_element_type=f32)
                    imag = lax.dot_general(turned, right, CONTRACT_LANES, preferred_element_type=f32)
                    upper = lax.broadcasted_iota(jnp.int32, (256, 256), 1) >= lax.broadcasted_iota(
                        jnp.int32, (256, 256), 0
                    )
                    finish(jnp.where(upper, real, imag))

                return c

            lax.fori_loop(0, 4, block, 0)
            if half == 1:
                pltpu.make_async_copy(visbuf.at[rows], vis.at[rows], vis_sem).start()
            return carry

        lax.fori_loop(0, 4, stripe, 0)

    distribute(0)

    core_copy.wait()

    def pack1(s, carry):
        row = pl.multiple_of((s * 2 + my_core) * 32, 32)
        total = beams[pl.ds(row, 32), :] + brecv0[s].astype(f32)
        beams[pl.ds(row, 32), :] = total
        bsend1[s % 4, s // 4] = total.astype(bf16)
        return carry

    lax.fori_loop(0, 32, pack1, 0)
    x_copies = []
    for d in range(1, 4):
        x = (my_x + d) % 4
        x_copies.append(
            pltpu.make_async_remote_copy(
                src_ref=bsend1.at[x], dst_ref=brecv1.at[d - 1],
                send_sem=bsend_sem.at[d], recv_sem=brecv_sem.at[d],
                **to({"af": my_z * 8 + x * 2 + my_core}),
            )
        )
        x_copies[-1].start()

    distribute(1)

    for copy in x_copies:
        copy.wait()

    def pack2(zz, carry):
        row = pl.multiple_of(((zz * 4 + my_x) * 2 + my_core) * 32, 32)
        total = beams[pl.ds(row, 32), :]
        for d in range(3):
            total = total + brecv1[d, zz].astype(f32)
        beams[pl.ds(row, 32), :] = total
        bsend2[zz] = total.astype(bf16)
        return carry

    lax.fori_loop(0, 8, pack2, 0)
    z_copies = []
    for d in range(1, 8):
        zz = (my_z + d) % 8
        z_copies.append(
            pltpu.make_async_remote_copy(
                src_ref=bsend2.at[zz], dst_ref=brecv2.at[d - 1],
                send_sem=bsend_sem.at[3 + d], recv_sem=brecv_sem.at[3 + d],
                **to({"af": zz * 8 + my_low}),
            )
        )
        z_copies[-1].start()

    correlate(0)

    for copy in z_copies:
        copy.wait()
    total = beams[pl.ds(pl.multiple_of(me * 32, 32), 32), :]
    for d in range(7):
        total = total + brecv2[d].astype(f32)
    square = total * total
    power[...] = square + pltpu.roll(square, 64, 1)

    correlate(1)
    for half in range(2):
        pltpu.make_async_copy(
            ysend.at[half, pl.ds(0, GROUPS - 1)], ysend.at[half, pl.ds(0, GROUPS - 1)], ysend_sem.at[half]
        ).wait()
        others = pl.ds(0, BINS - 1)
        pltpu.make_async_copy(outgo.at[half, others], outgo.at[half, others], send_sem.at[half]).wait()
    pltpu.make_async_copy(visbuf, vis, vis_sem).wait()


def beam_matrix(stations, weights, first_input):
    ids = (first_input + jnp.arange(LOCAL, dtype=jnp.int32)) // 2
    member = jnp.sum((stations[:, :, None] == ids[None, None, :]).astype(jnp.float32), axis=1)
    chosen = lax.dynamic_slice_in_dim(weights, first_input, LOCAL, 2)
    w = (member[None] * chosen).astype(jnp.bfloat16)
    w = jnp.pad(w, ((0, 0), (0, 8 - NB), (0, 0)))
    table = jnp.stack([jnp.stack([w[0], w[1]], 0), jnp.stack([-w[1], w[0]], 0)], 0)
    same = (jnp.arange(2 * HALF)[:, None] == jnp.arange(NT)[None, :]).reshape(2, 1, HALF, 1, 1, NT, 1)
    body = table.transpose(0, 3, 1, 2)[None, :, None, :, :, None, :]
    full = jnp.where(same, body, jnp.zeros((), jnp.bfloat16))
    return full.reshape(2, FINE, FINE)


def per_device(volts, history, pfb_taps, zoom_bins, counts, beam_stations, beam_weights):
    me = lax.axis_index("af")
    group = lax.axis_index("gx")
    bins_here = lax.dynamic_slice_in_dim(zoom_bins[:, 0], group * CHG, CHG)
    counts_here = lax.dynamic_slice_in_dim(counts, group * CHG, CHG)
    lane = jnp.arange(FINE, dtype=jnp.int32)[None, :]
    aux = jnp.where(
        lane < BINS,
        bins_here[:, None] == lane,
        jnp.logical_and(lane < 64 + NT, lane - 64 < counts_here[:, None]),
    ).astype(jnp.bfloat16)
    weights = beam_matrix(beam_stations, beam_weights, me * LOCAL)
    vmem = pl.BlockSpec(memory_space=pltpu.VMEM)
    hbm = pl.BlockSpec(memory_space=pl.ANY)
    bf16, f32 = jnp.bfloat16, jnp.float32
    dma = pltpu.SemaphoreType.DMA
    vis, power = pl.pallas_call(
        kernel,
        out_shape=[
            jax.ShapeDtypeStruct((NIN, NIN), bf16),
            jax.ShapeDtypeStruct((32, FINE), f32),
        ],
        in_specs=[hbm, hbm, vmem, vmem, vmem, vmem],
        out_specs=[hbm, vmem],
        scratch_shapes=[
            pltpu.VMEM((COARSE, NT + TAPS - 1, LOCAL, 2, FINE), bf16),
            pltpu.VMEM((HALF * 2 * LOCAL, FINE), f32),
            pltpu.VMEM((2, GROUPS, COARSE, 16, FINE), bf16),
            pltpu.VMEM((2, GROUPS, COARSE, 16, FINE), bf16),
            pltpu.VMEM((8, CHG, 512), bf16),
            pltpu.VMEM((2, BINS, LOCAL, LANES), bf16),
            pltpu.VMEM((2, NIN, LANES), bf16),
            pltpu.VMEM((4, 4, 256, 256), f32),
            pltpu.VMEM((NIN, NIN), bf16),
            pltpu.VMEM((CHG, FINE), f32),
            pltpu.VMEM((32, 32, FINE), bf16),
            pltpu.VMEM((32, 32, FINE), bf16),
            pltpu.VMEM((4, 8, 32, FINE), bf16),
            pltpu.VMEM((3, 8, 32, FINE), bf16),
            pltpu.VMEM((8, 32, FINE), bf16),
            pltpu.VMEM((7, 32, FINE), bf16),
            dma,
            dma((2,)),
            dma((2,)),
            dma((2,)),
            dma((2,)),
            dma((11,)),
            dma((11,)),
            dma,
        ],
        compiler_params=pltpu.CompilerParams(
            collective_id=0, has_side_effects=True, vmem_limit_bytes=56 * 1024 * 1024
        ),
    )(volts, history, aux, dft_rows(), pfb_taps, weights)
    beam_power = power[:, :64].reshape(2, COARSE, NT, 8)[..., :NB].transpose(3, 1, 0, 2)
    return vis[None, None], beam_power


def solution(mesh):
    in_specs = (P("af", "gx", None, None), P("af", "gx", None, None), P(), P(), P(), P(), P())
    out_specs = (P("af", "gx", None, None), P(None, "gx", "af", None))
    return jax.shard_map(
        per_device, mesh=mesh, in_specs=in_specs, out_specs=out_specs, check_vma=False
    )
```

time: 399 us -> 111 us (0.28); the launches traced: 393 us -> 111 us
  local copies, waits for them, and re-layouts: 174 us -> 6.45 us
  waiting for transfers between devices: 140 us -> 0 us
  Pallas kernels: 0 us -> 98.8 us
  starting transfers between devices: 23.7 us -> 0 us
  other arithmetic: 23 us -> 4.56 us
  matrix products: 17.3 us -> 0 us
  between operations: 14.9 us -> 0.77 us
    reduce_scatter x1 -> x0, waiting for transfers between devices: 138 us -> none  [per_device(): lax.psum_scatter(partial_beams, 'af', scatter_dimension=3, tiled=True)]
    pallas_call x0 -> x1, Pallas kernels: none -> 98.8 us  [per_device(): pl.pallas_call(kernel, out_shape=[jax.ShapeDtypeStruct((NIN, NIN), bf16),...]
    gather x4 -> x0, local copies, waits for them, and re-layouts: 68.3 us -> none  [the longest x2 55.8 us: per_device(): jnp.take(flat_group, source.reshape(-1), axis=3)]
    unnamed x11 -> x4, local copies, waits for them, and re-layouts: 31.3 us -> 3.71 us
    reshape x5 -> x1, local copies, waits for them, and re-layouts: 27.4 us -> 0.1 us  [per_device(): power[:, :64].reshape(2, COARSE, NT, 8)[..., :NB].transpose(3, 1, 0, 2)]
    all_to_all x2 -> x0, starting transfers between devices: 23.6 us -> none  [the longest x1 16 us: per_device(): lax.all_to_all(slots, 'af', split_axis=3, concat_axis=0, tiled=True)]
    dot_general x4 -> x0, matrix products: 17.3 us -> none  [the longest x1 11.9 us: per_device(): lax.dot_general(flat, flat, contract, preferred_element_type=jnp.float32)]
    scatter x2 -> x0, local copies, waits for them, and re-layouts: 16.5 us -> none  [the longest x1 8.28 us: slot_table(): jnp.zeros((bin_count * capacity,), jnp.int32).at[target]]
  transfers between devices with their start and end apart: 3 -> 0, of which waited for: 2 -> 0; matrix products, arithmetic and copies ran while one was open for 12% -> 0% of each run, Pallas kernels for 0% -> 0%
where the time goes in v1:
time: 111 us
  Pallas kernels  98.8 us (89%)
  local copies, waits for them, and re-layouts  6.45 us (6%)
  other arithmetic  4.56 us (4%)
    pallas_call x1, Pallas kernels, per_device(): pl.pallas_call(kernel, out_shape=[jax.ShapeDtypeStruct((NIN, NIN), bf16),...  98.8 us
    unnamed x4, local copies, waits for them, and re-layouts  3.71 us

profile of v1, /device:TPU:1, one launch (start us, length us, event | category | flops | bytes accessed | tf_op | source)
XLA Modules:
  0.0 110.6 jit_solution(9910085090268373063)
XLA Ops:
  0.6 0.0 copy-start
  0.7 0.9 convert_reduce_fusion
  1.6 0.8 multiply_convert_fusion
  2.4 0.0 copy-done
  2.4 0.7 dynamic_slice.10
  3.2 0.1 broadcast_in_dim.49
  3.3 0.2 broadcast_in_dim.50
  3.4 0.1 copy.18
  3.6 0.2 broadcast_in_dim.47
  3.8 0.4 broadcast_in_dim.48
  4.2 0.1 copy.19
  4.3 0.6 broadcast_select_fusion.weights
  4.9 2.2 %fusion.1.aux = bf16[2048,128]{1,0:T(8,128)(2,1)} fusion(s32[128]{0:T(128)S(1)} %iota_add_fusion, s32[2048]{0:T(1024)S(1)} %bitcast.18, s32[2048]{0:T(1024)S(1)} %dynamic_slice.10, pred[128]{0:T(512)(128)(4,1)S(1)} %get-tuple-element.12, pred[128]{0:T(512)(128)(4,1)S(1)} %get-tuple-element.13), kind=kLoop, calls=%fused_computation.2 | loop fusion | flops 1310720 | bytes 541440 | tf_op jit(solution)/shard_map/convert_element_type | solution.py:367
  7.2 98.8 %shard_map.95 = (bf16[1024,1024]{1,0:T(8,128)(2,1)}, f32[32,128]{1,0:T(8,128)}) custom-call(bf16[16,16,2,1024]{3,2,1,0:T(2,128)(2,1)} %volts.1, bf16[16,16,2,1408]{3,2,1,0:T(2,128)(2,1)} %history.1, bf16[2048,128]{1,0:T(8,128)(2,1)} %fusion.1.aux, bf16[128,256]{1,0:T(8,128)(2,1)} %constant.50.clone.table, f32[12,128]{1,0:T(8,128)} %taps.1, ...), custom_call_target="tpu_custom_call" | custom-call | tf_op jit(solution)/shard_map/pallas_call | solution.py:373
  106.0 0.8 copy.20
  106.8 0.1 reshape.69
  106.9 0.6 copy.21
  107.5 3.1 %copy.23 = bf16[1,1,1024,1024]{3,2,1,0:T(8,128)(2,1)} copy(bf16[1,1,1024,1024]{3,2,1,0:T(8,128)(2,1)} %bitcast.17) | data formatting | bytes 4194304
  (11 shorter events, 0.1 us)
Async XLA Ops:
  0.6 1.7 %copy-start = (s32[16384,1]{0,1:T(1,128)S(1)}, s32[16384,1]{0,1:T(1,128)}, u32[]{:S(2)}) copy-start(s32[16384,1]{0,1:T(1,128)} %param.11) | copy-start | bytes 196612

commit v2 on v1

v2 whole, which is shorter than its diff:
```python
import jax
import jax.numpy as jnp
import numpy as np
from jax import lax
from jax.experimental import pallas as pl
from jax.experimental.pallas import tpu as pltpu
from jax.sharding import PartitionSpec as P

FINE = 128
TAPS = 12
NT = 8
NB = 6
BINS = 64
GROUPS = 8
LOCAL = 16
COARSE = 16
CHG = 2048
NIN = 1024
STEPS = 4
LANES = 256
MESH = pl.DeviceIdType.MESH
CONTRACT_LANES = (((1,), (1,)), ((), ()))


def dft_rows():
    index = np.arange(FINE)
    angle = (index[:, None] * index[None, :] % FINE) * (2.0 * np.pi / FINE)
    cosine = np.cos(angle) / np.sqrt(FINE)
    sine = np.sin(angle) / np.sqrt(FINE)
    return jnp.asarray(np.concatenate([cosine.T, sine.T], axis=1), jnp.bfloat16)


def to(device):
    return dict(device_id=device, device_id_type=MESH)


def iota(shape, dim):
    return lax.broadcasted_iota(jnp.int32, shape, dim)


def kernel(
    volts, history, zoom_bins, counts, table, taps, stations, beam_weights,
    vis, power,
    frames, filt, ysend, yrecv, place, pick, limit, outgo, arrived, turned, acc, visbuf,
    wpad, beams, beams2, bsend0, brecv0, bsend1, brecv1, bsend2, brecv2,
    frame_sem, ysend_sem, yrecv_sem, send_sem, recv_sem,
    bsend_sem, brecv_sem, vis_sem,
):
    me = lax.axis_index("af")
    gx = lax.axis_index("gx")
    my_z = me // 8
    my_x = (me // 2) % 4
    my_core = me % 2
    my_low = me % 8
    f32, bf16 = jnp.float32, jnp.bfloat16

    barrier = pltpu.get_barrier_semaphore()

    def first_frame(step):
        return 0 if step == 0 else 11 + 2 * step

    def fetch_step(step):
        def one(i, carry):
            for f in range(first_frame(step), 13 + 2 * step):
                cut_fetch(f, i, step)
            return carry

        lax.fori_loop(0, LOCAL, one, 0)

    def cut_fetch(f, i, step):
        if f < TAPS - 1:
            source = history.at[i, :, :, f * FINE : (f + 1) * FINE]
        else:
            source = volts.at[i, :, :, (f - TAPS + 1) * FINE : (f - TAPS + 2) * FINE]
        pltpu.make_async_copy(source, frames.at[f, :, pl.ds(2 * i, 2)], frame_sem.at[step]).start()

    fetch_step(0)

    def greet(d, carry):
        pl.semaphore_signal(barrier, inc=1, **to({"af": (me + d) % BINS}))
        return carry

    lax.fori_loop(1, BINS, greet, 0)

    def greet_gx(d, carry):
        pl.semaphore_signal(barrier, inc=1, **to({"gx": (gx + d) % GROUPS}))
        return carry

    lax.fori_loop(1, GROUPS, greet_gx, 0)
    for step in range(1, STEPS):
        fetch_step(step)

    def channelize(step):
        cut = frames.at[first_frame(step) : 13 + 2 * step]
        pltpu.make_async_copy(cut, cut, frame_sem.at[step]).wait()

        def bank(c, carry):
            for part in range(2):
                rows = slice(part * LOCAL, (part + 1) * LOCAL)
                x = [frames[2 * step + j, c, rows, :].astype(f32) for j in range(TAPS + 1)]
                for t in range(2):
                    total = x[t] * taps[0:1, :]
                    for j in range(1, TAPS):
                        total = total + x[t + j] * taps[j : j + 1, :]
                    filt[c, t * 32 + part * LOCAL : t * 32 + (part + 1) * LOCAL, :] = total
            return carry

        lax.fori_loop(0, COARSE, bank, 0, unroll=2)

        def transform(u, carry):
            blocks = []
            for cp in range(2):
                for upper in range(2):
                    c = 2 * u + cp + 8 * upper
                    re = filt[c, pl.ds(0, 32, stride=2), :].astype(bf16)
                    im = filt[c, pl.ds(1, 32, stride=2), :].astype(bf16)
                    blocks.append(jnp.concatenate([re, im], axis=1))
                    blocks.append(jnp.concatenate([im, -re], axis=1))
            rows = jnp.concatenate(blocks, axis=0)
            spectra = lax.dot_general(table[...], rows, CONTRACT_LANES, preferred_element_type=f32).astype(bf16)
            for cp in range(2):
                ysend[step, :, 2 * u + cp] = spectra[:, cp * FINE : (cp + 1) * FINE].reshape(GROUPS, 16, FINE)
            return carry

        lax.fori_loop(0, 4, transform, 0, unroll=2)

    def send_spectra(step):
        def one(d, carry):
            dest = (gx + d) % GROUPS
            pltpu.make_async_remote_copy(
                src_ref=ysend.at[step, dest],
                dst_ref=yrecv.at[step, gx],
                send_sem=ysend_sem.at[step],
                recv_sem=yrecv_sem.at[step],
                **to({"gx": dest}),
            ).start()
            return carry

        lax.fori_loop(1, GROUPS, one, 0)
        yrecv[step, gx] = ysend[step, gx]

    channelize(0)
    pl.semaphore_wait(barrier, BINS - 1 + GROUPS - 1)
    send_spectra(0)
    channelize(1)
    send_spectra(1)

    my_rows = pl.ds(pl.multiple_of(gx * 16, 16), 16)
    bins_here = zoom_bins[my_rows, :]
    counts_here = counts[my_rows, :]
    in_bin = jnp.where(bins_here == me, counts_here.astype(f32), 0.0)
    in_bin = jnp.sum(jnp.sum(in_bin, axis=1, keepdims=True), axis=0, keepdims=True)
    scale = 1.0 / jnp.maximum(in_bin, 1.0)
    bins_down = bins_here.astype(f32).T
    counts_down = counts_here.astype(f32).T
    lane = iota((FINE, FINE), 1)
    lane_f = lane.astype(f32)
    lower = (lane < iota((FINE, FINE), 0)).astype(f32).astype(bf16)
    ones = jnp.ones((FINE, FINE), bf16)
    seen = jnp.zeros((1, FINE), f32)
    for block in range(16):
        upper, y = block // 8, block % 8
        row = 2 * y + upper
        column = jnp.broadcast_to(bins_down[:, row : row + 1], (FINE, FINE))
        hits = (column == lane_f).astype(f32)
        before = jnp.dot(lower, hits.astype(bf16), preferred_element_type=f32) + seen
        seen = seen + jnp.sum(hits, axis=0, keepdims=True)
        rank = jnp.dot((hits * before).astype(bf16), ones, preferred_element_type=f32)
        pair = jnp.floor(column * 0.5)
        slot = (column - 2.0 * pair) * 64.0 + rank
        place[block * FINE : (block + 1) * FINE, :] = jnp.where(slot == lane_f, pair, -1.0).astype(bf16)

    def spread(z, carry):
        for p in range(4):
            here = (z * 4 + p).astype(f32).astype(bf16)
            pick[z, :, p * FINE : (p + 1) * FINE] = jnp.where(
                place[...] == here, jnp.ones((), bf16), jnp.zeros((), bf16)
            )
        return carry

    lax.fori_loop(0, 8, spread, 0)
    for y in range(8):
        first = jnp.broadcast_to(counts_down[:, 2 * y : 2 * y + 1], (FINE, FINE))
        second = jnp.broadcast_to(counts_down[:, 2 * y + 1 : 2 * y + 2], (FINE, FINE))
        limit[y * FINE : (y + 1) * FINE, :] = jnp.where(lane < 64, first, second)

    own_rows = pl.ds(pl.multiple_of(me * LOCAL, LOCAL), LOCAL)

    def distribute(step):
        others = pl.ds(0, GROUPS - 1)
        pltpu.make_async_copy(yrecv.at[step, others], yrecv.at[step, others], yrecv_sem.at[step]).wait()
        spectrum = 2 * step + (iota((FINE, FINE), 1) // LOCAL) % 2
        pieces = []
        for y in range(GROUPS):
            samples = yrecv[step, y].reshape(FINE, FINE).astype(f32)
            keep = spectrum.astype(f32) < limit[y * FINE : (y + 1) * FINE, :]
            pieces.append(jnp.where(keep, samples, 0.0).T.astype(bf16))
        flipped = jnp.concatenate([p[:64] for p in pieces] + [p[64:] for p in pieces], axis=1)
        low = iota((LOCAL, FINE), 1) < 64

        def one(turn, carry):
            turn = 7 - turn
            hop = ((turn + 1) // 2) * (2 * (turn % 2) - 1)
            z = (my_z + hop + 8) % 8
            picked = jnp.dot(flipped, pick[z], preferred_element_type=f32)
            for pair in range(4):
                for s in range(2):
                    first = picked[s * 32 : s * 32 + 16, pair * FINE : (pair + 1) * FINE]
                    second = picked[s * 32 + 16 : s * 32 + 32, pair * FINE : (pair + 1) * FINE]
                    second = pltpu.roll(second, 64, 1)
                    cols = slice(s * FINE, (s + 1) * FINE)
                    outgo[step, z * 8 + 2 * pair, :, cols] = jnp.where(low, first, second).astype(bf16)
                    outgo[step, z * 8 + 2 * pair + 1, :, cols] = jnp.where(low, second, first).astype(bf16)

            def send(k, c):
                dest = z * 8 + (my_low + k) % 8

                @pl.when(dest != me)
                def _():
                    pltpu.make_async_remote_copy(
                        src_ref=outgo.at[step, dest],
                        dst_ref=arrived.at[step, own_rows],
                        send_sem=send_sem.at[step],
                        recv_sem=recv_sem.at[step],
                        **to({"af": dest}),
                    ).start()

                return c

            lax.fori_loop(0, 8, send, 0)
            return carry

        lax.fori_loop(0, 8, one, 0, unroll=8)
        arrived[step, own_rows] = outgo[step, me]

    distribute(0)
    channelize(2)
    send_spectra(2)
    channelize(3)
    send_spectra(3)
    distribute(1)

    lanes6 = iota((NB, FINE), 1)
    member = jnp.zeros((NB, FINE), f32)
    for st in range(LOCAL // 2):
        found = jnp.sum((stations[...] == me * (LOCAL // 2) + st).astype(f32), axis=1, keepdims=True)
        member = jnp.where(lanes6 // 2 == st, found, member)
    wpad[...] = jnp.zeros_like(wpad)
    for p in range(2):
        piece = beam_weights[p, :, pl.ds(pl.multiple_of((me // 8) * FINE, FINE), FINE)]
        piece = pltpu.roll(piece, (FINE - my_low * LOCAL) % FINE, 1)
        wpad[p * 8 : p * 8 + NB, :] = member * piece
    by_input = (iota((512, FINE), 1) == iota((512, FINE), 0) % LOCAL).astype(f32).astype(bf16)
    chosen = lax.dot_general(by_input, wpad[...].astype(bf16), CONTRACT_LANES, preferred_element_type=f32)
    chosen = chosen.astype(bf16)
    wide_row, wide_lane = iota((16, 256), 0), iota((16, 256), 1)
    wre = jnp.dot(chosen, (wide_row == wide_lane % 8).astype(f32).astype(bf16), preferred_element_type=f32)
    wim = jnp.dot(chosen, (wide_row == 8 + wide_lane % 8).astype(f32).astype(bf16), preferred_element_type=f32)
    row, col = iota((512, 256), 0), iota((512, 256), 1)
    s_of, part_of = (row // 32) % 2, (col // 64) % 2
    same = jnp.logical_and(
        (row // 64) % 2 == col // 128, 2 * (row // 128) + (row // LOCAL) % 2 == (col // 8) % 8
    )
    mixed = jnp.where(s_of == part_of, wre, jnp.where(s_of == 0, wim, -wim))
    weights = jnp.where(same, mixed, 0.0).astype(bf16)
    for z in range(8):
        spectra = jnp.concatenate([ysend[step, z].reshape(FINE, FINE) for step in range(STEPS)], axis=1)
        whole = jnp.dot(spectra, weights, preferred_element_type=f32)
        beams[0] = whole[:, :FINE]
        beams[1] = whole[:, FINE:]
        for x in range(4):
            for core in range(2):
                for e in range(2):
                    for h in range(2):
                        beams2[z, x, core, e * 8 : e * 8 + 8, h * FINE : (h + 1) * FINE] = beams[
                            h, pl.ds(x * 4 + core * 2 + e, 8, stride=16), :
                        ]

    def pack0(s, carry):
        bsend0[s] = beams2[s // 4, s % 4, 1 - my_core].astype(bf16)
        return carry

    lax.fori_loop(0, 32, pack0, 0)
    sibling = my_z * 8 + my_x * 2 + 1 - my_core
    core_copy = pltpu.make_async_remote_copy(
        src_ref=bsend0, dst_ref=brecv0, send_sem=bsend_sem.at[0], recv_sem=brecv_sem.at[0],
        **to({"af": sibling}),
    )
    core_copy.start()

    distribute(2)

    core_copy.wait()

    def pack1(s, carry):
        total = beams2[s // 4, s % 4, my_core] + brecv0[s].astype(f32)
        beams2[s // 4, s % 4, my_core] = total
        bsend1[s % 4, s // 4] = total.astype(bf16)
        return carry

    lax.fori_loop(0, 32, pack1, 0)
    x_copies = []
    for d in range(1, 4):
        x = (my_x + d) % 4
        x_copies.append(
            pltpu.make_async_remote_copy(
                src_ref=bsend1.at[x], dst_ref=brecv1.at[d - 1],
                send_sem=bsend_sem.at[d], recv_sem=brecv_sem.at[d],
                **to({"af": my_z * 8 + x * 2 + my_core}),
            )
        )
        x_copies[-1].start()

    distribute(3)

    for copy in x_copies:
        copy.wait()

    def pack2(zz, carry):
        total = beams2[zz, my_x, my_core]
        for d in range(3):
            total = total + brecv1[d, zz].astype(f32)
        beams2[zz, my_x, my_core] = total
        bsend2[zz] = total.astype(bf16)
        return carry

    lax.fori_loop(0, 8, pack2, 0)
    z_copies = []
    for d in range(1, 8):
        zz = (my_z + d) % 8
        z_copies.append(
            pltpu.make_async_remote_copy(
                src_ref=bsend2.at[zz], dst_ref=brecv2.at[d - 1],
                send_sem=bsend_sem.at[3 + d], recv_sem=brecv_sem.at[3 + d],
                **to({"af": zz * 8 + my_low}),
            )
        )
        z_copies[-1].start()

    diagonal = iota((256, 256), 1) >= iota((256, 256), 0)

    def correlate(step, last):
        others = pl.ds(0, (BINS - 1) * LOCAL)
        pltpu.make_async_copy(arrived.at[step, others], arrived.at[step, others], recv_sem.at[step]).wait()
        turned[:, :FINE] = arrived[step, :, FINE:]
        turned[:, FINE:] = -arrived[step, :, :FINE]
        for bi in range(4):
            rows = slice(bi * 256, (bi + 1) * 256)
            for bj in range(4):
                cols = slice(bj * 256, (bj + 1) * 256)
                right = arrived[step, cols, :]
                if bj >= bi:
                    real = lax.dot_general(
                        arrived[step, rows, :], right, CONTRACT_LANES, preferred_element_type=f32
                    )
                if bj <= bi:
                    imag = lax.dot_general(turned[rows, :], right, CONTRACT_LANES, preferred_element_type=f32)
                if bj > bi:
                    value = real
                elif bj < bi:
                    value = imag
                else:
                    value = jnp.where(diagonal, real, imag)
                if last:
                    visbuf[rows, cols] = ((acc[bi, bj] + value) * scale).astype(bf16)
                else:
                    acc[bi, bj] = acc[bi, bj] + value
            if last:
                pltpu.make_async_copy(visbuf.at[rows], vis.at[rows], vis_sem).start()

    def clear(k, carry):
        acc[k // 4, k % 4] = jnp.zeros((256, 256), f32)
        return carry

    lax.fori_loop(0, 16, clear, 0)

    def early(step, carry):
        correlate(step, False)
        return carry

    lax.fori_loop(0, STEPS - 1, early, 0)

    for copy in z_copies:
        copy.wait()
    total = beams2[my_z, my_x, my_core]
    for d in range(7):
        total = total + brecv2[d].astype(f32)
    square = total * total
    for h in range(2):
        half = square[:, h * FINE : (h + 1) * FINE]
        power[:, h * FINE : (h + 1) * FINE] = half + pltpu.roll(half, 64, 1)

    correlate(STEPS - 1, True)
    for step in range(STEPS):
        others = pl.ds(0, GROUPS - 1)
        pltpu.make_async_copy(ysend.at[step, others], ysend.at[step, others], ysend_sem.at[step]).wait()
        others = pl.ds(0, BINS - 1)
        pltpu.make_async_copy(outgo.at[step, others], outgo.at[step, others], send_sem.at[step]).wait()
    pltpu.make_async_copy(visbuf, vis, vis_sem).wait()


def per_device(volts, history, pfb_taps, zoom_bins, counts, beam_stations, beam_weights):
    vmem = pl.BlockSpec(memory_space=pltpu.VMEM)
    hbm = pl.BlockSpec(memory_space=pl.ANY)
    bf16, f32 = jnp.bfloat16, jnp.float32
    dma = pltpu.SemaphoreType.DMA
    vis, power = pl.pallas_call(
        kernel,
        out_shape=[
            jax.ShapeDtypeStruct((NIN, NIN), bf16),
            jax.ShapeDtypeStruct((16, 2 * FINE), f32),
        ],
        in_specs=[hbm, hbm, vmem, vmem, vmem, vmem, vmem, vmem],
        out_specs=[hbm, vmem],
        scratch_shapes=[
            pltpu.VMEM((NT + TAPS - 1, COARSE, 2 * LOCAL, FINE), bf16),
            pltpu.VMEM((COARSE, 64, FINE), f32),
            pltpu.VMEM((STEPS, GROUPS, 8, 16, FINE), bf16),
            pltpu.VMEM((STEPS, GROUPS, 8, 16, FINE), bf16),
            pltpu.VMEM((CHG, FINE), bf16),
            pltpu.VMEM((8, CHG, 512), bf16),
            pltpu.VMEM((CHG // 2, FINE), f32),
            pltpu.VMEM((STEPS, BINS, LOCAL, LANES), bf16),
            pltpu.VMEM((STEPS, NIN, LANES), bf16),
            pltpu.VMEM((NIN, LANES), bf16),
            pltpu.VMEM((4, 4, 256, 256), f32),
            pltpu.VMEM((NIN, NIN), bf16),
            pltpu.VMEM((16, FINE), f32),
            pltpu.VMEM((2, FINE, FINE), f32),
            pltpu.VMEM((8, 4, 2, 16, 256), f32),
            pltpu.VMEM((32, 16, 256), bf16),
            pltpu.VMEM((32, 16, 256), bf16),
            pltpu.VMEM((4, 8, 16, 256), bf16),
            pltpu.VMEM((3, 8, 16, 256), bf16),
            pltpu.VMEM((8, 16, 256), bf16),
            pltpu.VMEM((7, 16, 256), bf16),
            dma((STEPS,)),
            dma((STEPS,)),
            dma((STEPS,)),
            dma((STEPS,)),
            dma((STEPS,)),
            dma((11,)),
            dma((11,)),
            dma,
        ],
        compiler_params=pltpu.CompilerParams(
            collective_id=0, has_side_effects=True, vmem_limit_bytes=56 * 1024 * 1024
        ),
    )(
        volts, history, zoom_bins.reshape(FINE, FINE), counts.reshape(FINE, FINE),
        dft_rows(), pfb_taps, beam_stations, beam_weights,
    )
    split = power.reshape(2, 8, 2, 2, NT, 8)[:, :, :, 0, :, :NB]
    beam_power = split.transpose(4, 2, 1, 0, 3).reshape(NB, COARSE, 2, NT)
    return vis[None, None], beam_power


def solution(mesh):
    in_specs = (P("af", "gx", None, None), P("af", "gx", None, None), P(), P(), P(), P(), P())
    out_specs = (P("af", "gx", None, None), P(None, "gx", "af", None))
    return jax.shard_map(
        per_device, mesh=mesh, in_specs=in_specs, out_specs=out_specs, check_vma=False
    )
```

time: 111 us -> 87.9 us (0.79)
  Pallas kernels: 98.8 us -> 80.4 us
  other arithmetic: 4.56 us -> 0 us
    pallas_call x1, Pallas kernels: 98.8 us -> 80.4 us  [per_device(): pl.pallas_call(kernel, out_shape=[jax.ShapeDtypeStruct((NIN, NIN), bf16),...]
    convert_element_type x2 -> x0, other arithmetic: 2.98 us -> none  [the longest x1 2.21 us: per_device(): aux = jnp.where(lane < BINS, bins_here[:, None] == lane, jnp.logical_and(...]
    reshape x1 -> x2, local copies, waits for them, and re-layouts: 0.1 us -> 1.61 us  [the longest x1 0.87 us: per_device(): split = power.reshape(2, 8, 2, 2, NT, 8)[:, :, :, 0, :, :NB]]
    broadcast_in_dim x6 -> x0, local copies, waits for them, and re-layouts: 1.11 us -> none  [beam_matrix(): full = jnp.where(same, body, jnp.zeros((), jnp.bfloat16))]
    unnamed x4 -> x2, local copies, waits for them, and re-layouts: 3.71 us -> 4.53 us
where the time goes in v2:
time: 87.9 us; the launch traced here: 87.6 us
  Pallas kernels  80.4 us (91%)
  local copies, waits for them, and re-layouts  6.48 us (7%)
    pallas_call x1, Pallas kernels, per_device(): pl.pallas_call(kernel, out_shape=[jax.ShapeDtypeStruct((NIN, NIN), bf16),...  80.4 us
    unnamed x2, local copies, waits for them, and re-layouts  4.53 us

profile of v2, /device:TPU:1, one launch (start us, length us, event | category | flops | bytes accessed | tf_op | source)
XLA Modules:
  0.0 87.6 jit_solution(4032765256950977426)
XLA Ops:
  0.6 1.4 %copy.10.beam_weights = f32[2,6,1024]{2,1,0:T(8,128)} copy(f32[2,6,1024]{2,0,1:T(2,128)} %param.14) | data formatting | bytes 98304 | tf_op args[6]
  2.1 80.4 %shard_map.95 = (bf16[1024,1024]{1,0:T(8,128)(2,1)}, f32[16,256]{1,0:T(8,128)}) custom-call(bf16[16,16,2,1024]{3,2,1,0:T(2,128)(2,1)} %volts.1, bf16[16,16,2,1408]{3,2,1,0:T(2,128)(2,1)} %history.1, s32[128,128]{1,0:T(8,128)} %bitcast.10, s32[128,128]{1,0:T(8,128)} %bitcast.11, bf16[128,256]{1,0:T(8,128)(2,1)} %constant.2.clone.table, f32[12,128]{1,0:T(8,128)} %taps.1, ...), custom_call_target="tpu_custom_call" | custom-call | tf_op jit(solution)/shard_map/pallas_call | solution.py:407
  82.5 0.9 reshape.18
  83.4 0.3 copy.11
  83.7 0.7 reshape.19
  84.5 3.1 %copy.13 = bf16[1,1,1024,1024]{3,2,1,0:T(8,128)(2,1)} copy(bf16[1,1,1024,1024]{3,2,1,0:T(8,128)(2,1)} %bitcast.9) | data formatting | bytes 4194304
  (1 shorter events, 0.0 us)

commit v3 on v2

v3 whole, which is shorter than its diff:
```python
import jax
import jax.numpy as jnp
import numpy as np
from jax import lax
from jax.experimental import pallas as pl
from jax.experimental.pallas import tpu as pltpu
from jax.sharding import PartitionSpec as P

FINE = 128
TAPS = 12
NT = 8
NB = 6
BINS = 64
GROUPS = 8
LOCAL = 16
COARSE = 16
CHG = 2048
NIN = 1024
LANES = 256
PAIRS = 4
PARTS = ((0, 1), (1, 1), (2, 2), (4, 2), (6, 2))
STEPS = len(PARTS)
MESH = pl.DeviceIdType.MESH
CONTRACT_LANES = (((1,), (1,)), ((), ()))


def dft_rows():
    index = np.arange(FINE)
    angle = (index[:, None] * index[None, :] % FINE) * (2.0 * np.pi / FINE)
    cosine = np.cos(angle) / np.sqrt(FINE)
    sine = np.sin(angle) / np.sqrt(FINE)
    return jnp.asarray(np.concatenate([cosine.T, sine.T], axis=1), jnp.bfloat16)


def to(device):
    return dict(device_id=device, device_id_type=MESH)


def iota(shape, dim):
    return lax.broadcasted_iota(jnp.int32, shape, dim)


def kernel(
    volts, history, zoom_bins, counts, table, taps, stations, beam_weights,
    acc_out, last, beam_out, scale_out,
    frames, filt, ysend, yrecv, place, pick, outgo, arrived, turned, acc,
    wraw, member, beams, beams2, bsend0, brecv0, bsend1, brecv1, bsend2, brecv2,
    frame_sem, ysend_sem, yrecv_sem, send_sem, recv_sem,
    bsend_sem, brecv_sem, own_sem, acc_sem,
):
    me = lax.axis_index("af")
    gx = lax.axis_index("gx")
    my_z = me // 8
    my_x = (me // 2) % 4
    my_core = me % 2
    my_low = me % 8
    f32, bf16 = jnp.float32, jnp.bfloat16

    barrier = pltpu.get_barrier_semaphore()

    def frame_range(step):
        first, count = PARTS[step]
        return (first + TAPS - 1 if step else 0), first + count + TAPS - 1

    def fetch_step(step):
        def one(i, carry):
            for f in range(*frame_range(step)):
                if f < TAPS - 1:
                    source = history.at[i, :, :, f * FINE : (f + 1) * FINE]
                else:
                    source = volts.at[i, :, :, (f - TAPS + 1) * FINE : (f - TAPS + 2) * FINE]
                pltpu.make_async_copy(source, frames.at[f, :, pl.ds(2 * i, 2)], frame_sem.at[step]).start()
            return carry

        lax.fori_loop(0, LOCAL, one, 0)

    fetch_step(0)

    def greet(d, carry):
        pl.semaphore_signal(barrier, inc=1, **to({"af": (me + d) % BINS}))
        return carry

    lax.fori_loop(1, BINS, greet, 0)

    def greet_gx(d, carry):
        pl.semaphore_signal(barrier, inc=1, **to({"gx": (gx + d) % GROUPS}))
        return carry

    lax.fori_loop(1, GROUPS, greet_gx, 0)
    for step in range(1, STEPS):
        fetch_step(step)

    def channelize(step):
        first, count = PARTS[step]
        start, stop = frame_range(step)
        arrived_now = frames.at[start:stop]
        pltpu.make_async_copy(arrived_now, arrived_now, frame_sem.at[step]).wait()

        def bank(c, carry):
            for part in range(2):
                rows = slice(part * LOCAL, (part + 1) * LOCAL)
                x = [frames[first + j, c, rows, :].astype(f32) for j in range(TAPS + count - 1)]
                for t in range(count):
                    total = x[t] * taps[0:1, :]
                    for j in range(1, TAPS):
                        total = total + x[t + j] * taps[j : j + 1, :]
                    filt[c, t * 32 + part * LOCAL : t * 32 + (part + 1) * LOCAL, :] = total
            return carry

        lax.fori_loop(0, COARSE, bank, 0, unroll=2)
        span = 4 * count

        def transform(u, carry):
            blocks = []
            for cp in range(2):
                for q in range(COARSE // span):
                    c = 2 * u + cp + span * q
                    re = filt[c, pl.ds(0, count * LOCAL, stride=2), :].astype(bf16)
                    im = filt[c, pl.ds(1, count * LOCAL, stride=2), :].astype(bf16)
                    blocks.append(jnp.concatenate([re, im], axis=1))
                    blocks.append(jnp.concatenate([im, -re], axis=1))
            rows = jnp.concatenate(blocks, axis=0)
            spectra = lax.dot_general(table[...], rows, CONTRACT_LANES, preferred_element_type=f32).astype(bf16)
            for cp in range(2):
                ysend[first // 2, :, 4 * (first % 2) + 2 * u + cp] = spectra[
                    :, cp * FINE : (cp + 1) * FINE
                ].reshape(GROUPS, 16, FINE)
            return carry

        lax.fori_loop(0, span // 2, transform, 0, unroll=2)

    def y_part(ref, step, who):
        first, count = PARTS[step]
        return ref.at[first // 2, who, pl.ds(4 * (first % 2), 4 * count)]

    def send_spectra(step):
        first, count = PARTS[step]

        def one(d, carry):
            dest = (gx + d) % GROUPS
            pltpu.make_async_remote_copy(
                src_ref=y_part(ysend, step, dest),
                dst_ref=y_part(yrecv, step, gx),
                send_sem=ysend_sem.at[step],
                recv_sem=yrecv_sem.at[step],
                **to({"gx": dest}),
            ).start()
            return carry

        lax.fori_loop(1, GROUPS, one, 0)
        rows = slice(4 * (first % 2), 4 * (first % 2) + 4 * count)
        yrecv[first // 2, gx, rows] = ysend[first // 2, gx, rows]

    channelize(0)
    pl.semaphore_wait(barrier, BINS - 1 + GROUPS - 1)
    send_spectra(0)
    channelize(1)
    send_spectra(1)
    channelize(2)
    send_spectra(2)

    my_rows = pl.ds(pl.multiple_of(gx * 16, 16), 16)
    bins_here = zoom_bins[my_rows, :]
    counts_here = counts[my_rows, :]
    in_bin = jnp.where(bins_here == me, counts_here.astype(f32), 0.0)
    in_bin = jnp.sum(jnp.sum(in_bin, axis=1, keepdims=True), axis=0, keepdims=True)
    scale_out[...] = jnp.broadcast_to(1.0 / jnp.maximum(in_bin, 1.0), (8, FINE))
    bins_down = bins_here.astype(f32).T
    lane = iota((FINE, FINE), 1)
    lane_f = lane.astype(f32)
    lower = (lane < iota((FINE, FINE), 0)).astype(f32).astype(bf16)
    ones = jnp.ones((FINE, FINE), bf16)
    seen = jnp.zeros((1, FINE), f32)
    for block in range(16):
        upper, y = block // 8, block % 8
        row = 2 * y + upper
        column = jnp.broadcast_to(bins_down[:, row : row + 1], (FINE, FINE))
        hits = (column == lane_f).astype(f32)
        before = jnp.dot(lower, hits.astype(bf16), preferred_element_type=f32) + seen
        seen = seen + jnp.sum(hits, axis=0, keepdims=True)
        rank = jnp.dot((hits * before).astype(bf16), ones, preferred_element_type=f32)
        pair = jnp.floor(column * 0.5)
        slot = (column - 2.0 * pair) * 64.0 + rank
        place[block * FINE : (block + 1) * FINE, :] = jnp.where(slot == lane_f, pair, -1.0).astype(bf16)

    def spread(z, carry):
        for p in range(4):
            here = (z * 4 + p).astype(f32).astype(bf16)
            pick[z, :, p * FINE : (p + 1) * FINE] = jnp.where(
                place[...] == here, jnp.ones((), bf16), jnp.zeros((), bf16)
            )
        return carry

    lax.fori_loop(0, 8, spread, 0)
    own_rows = pl.ds(pl.multiple_of(me * LOCAL, LOCAL), LOCAL)

    def landing(step, rows):
        first, count = PARTS[step]
        cols = slice((first % 2) * FINE, (first % 2 + count) * FINE)
        if first // 2 == PAIRS - 1:
            return last.at[rows]
        return arrived.at[first // 2, rows, cols]

    def leaving(step, who):
        first, count = PARTS[step]
        cols = slice((first % 2) * FINE, (first % 2 + count) * FINE)
        return outgo.at[first // 2, who, :, cols]

    def distribute(step):
        first, count = PARTS[step]
        pair = first // 2
        others = y_part(yrecv, step, pl.ds(0, GROUPS - 1))
        pltpu.make_async_copy(others, others, yrecv_sem.at[step]).wait()
        spectrum = first + (iota((count * 32, FINE), 0) // LOCAL) % count
        cells = [[], []]
        for y in range(GROUPS):
            rows = slice(4 * (first % 2), 4 * (first % 2) + 4 * count)
            samples = yrecv[pair, y, rows].reshape(64 * count, FINE).astype(f32).T
            for upper in range(2):
                if count == 2:
                    cell = samples[upper * 64 : (upper + 1) * 64]
                else:
                    cell = jnp.concatenate(
                        [samples[q * 32 : (q + 1) * 32] for q in (2 * upper, 2 * upper + 1)], axis=1
                    )
                keep = spectrum < counts_here[2 * y + upper : 2 * y + upper + 1, :]
                cells[upper].append(jnp.where(keep, cell, 0.0).astype(bf16))
        flipped = jnp.concatenate(cells[0] + cells[1], axis=1)
        low = iota((LOCAL, FINE), 1) < 64

        def one(turn, carry):
            turn = 7 - turn
            hop = ((turn + 1) // 2) * (2 * (turn % 2) - 1)
            z = (my_z + hop + 8) % 8
            picked = jnp.dot(flipped, pick[z], preferred_element_type=f32)
            for b in range(4):
                for t in range(count):
                    lanes = slice(b * FINE, (b + 1) * FINE)
                    re = picked[t * 16 : t * 16 + 16, lanes]
                    im = picked[(count + t) * 16 : (count + t) * 16 + 16, lanes]
                    im = pltpu.roll(im, 64, 1)
                    cols = slice((first % 2 + t) * FINE, (first % 2 + t + 1) * FINE)
                    outgo[pair, z * 8 + 2 * b, :, cols] = jnp.where(low, re, im).astype(bf16)
                    outgo[pair, z * 8 + 2 * b + 1, :, cols] = jnp.where(low, im, re).astype(bf16)

            def send(k, c):
                dest = z * 8 + (my_low + k) % 8

                @pl.when(dest != me)
                def _():
                    pltpu.make_async_remote_copy(
                        src_ref=leaving(step, dest),
                        dst_ref=landing(step, own_rows),
                        send_sem=send_sem.at[step],
                        recv_sem=recv_sem.at[step],
                        **to({"af": dest}),
                    ).start()

                return c

            lax.fori_loop(0, 8, send, 0)
            return carry

        lax.fori_loop(0, 8, one, 0, unroll=8)
        if pair < PAIRS - 1:
            cols = slice((first % 2) * FINE, (first % 2 + count) * FINE)
            arrived[pair, own_rows, cols] = outgo[pair, me, :, cols]
        else:
            pltpu.make_async_copy(outgo.at[pair, me], last.at[own_rows], own_sem).start()

    def await_part(step):
        others = landing(step, pl.ds(0, (BINS - 1) * LOCAL))
        pltpu.make_async_copy(others, others, recv_sem.at[step]).wait()

    distribute(0)
    distribute(1)
    channelize(3)
    send_spectra(3)
    channelize(4)
    send_spectra(4)
    distribute(2)

    lanes6 = iota((NB, FINE), 1)
    found = jnp.zeros((NB, FINE), f32)
    for st in range(LOCAL // 2):
        here = jnp.sum((stations[...] == me * (LOCAL // 2) + st).astype(f32), axis=1, keepdims=True)
        found = jnp.where(lanes6 // 2 == st, here, found)
    wraw[...] = jnp.zeros_like(wraw)
    member[...] = jnp.zeros_like(member)
    near = pl.ds(pl.multiple_of((me // 8) * FINE, FINE), FINE)
    for p in range(2):
        member[p * 8 : p * 8 + NB, :] = found
        for b in range(NB):
            wraw[p * 8 + b : p * 8 + b + 1, :] = beam_weights[b, p : p + 1, near]
    by_beam = (member[...] * pltpu.roll(wraw[...], (FINE - my_low * LOCAL) % FINE, 1)).astype(bf16)

    def spread_weights(height, width, s_of, t_of, q_of):
        row, col = iota((height, width), 0), iota((height, width), 1)
        by_input = (iota((height, FINE), 1) == iota((height, FINE), 0) % LOCAL).astype(f32).astype(bf16)
        chosen = lax.dot_general(by_input, by_beam, CONTRACT_LANES, preferred_element_type=f32).astype(bf16)
        wide_row, wide_lane = iota((16, width), 0), iota((16, width), 1)
        beam = (wide_lane // 8) % 8
        wre = jnp.dot(chosen, (wide_row == beam).astype(f32).astype(bf16), preferred_element_type=f32)
        wim = jnp.dot(chosen, (wide_row == 8 + beam).astype(f32).astype(bf16), preferred_element_type=f32)
        same = jnp.logical_and(q_of(row) == col // FINE, t_of(row) == col % 8)
        mixed = jnp.where(s_of(row) == (col // 64) % 2, wre, jnp.where(s_of(row) == 0, wim, -wim))
        return jnp.where(same, mixed, 0.0).astype(bf16)

    early_weights = spread_weights(
        256, 512, lambda r: (r // 16) % 2, lambda r: r // 128, lambda r: (r // 32) % 4
    )
    late_weights = spread_weights(
        384, 256, lambda r: (r // 32) % 2, lambda r: 2 + 2 * (r // 128) + (r // 16) % 2, lambda r: (r // 64) % 2
    )
    for z in range(8):
        spectra = jnp.concatenate([ysend[p, z].reshape(FINE, FINE) for p in range(1, PAIRS)], axis=1)
        late = jnp.dot(spectra, late_weights, preferred_element_type=f32)
        spectra = jnp.concatenate([ysend[0, z, 4 * t : 4 * t + 4].reshape(64, FINE) for t in range(2)], axis=1)
        early = jnp.dot(spectra, early_weights, preferred_element_type=f32)
        for h in range(2):
            for low in range(2):
                rows = slice(low * 64, (low + 1) * 64)
                q = 2 * h + low
                beams[h, rows, :] = late[rows, h * FINE : (h + 1) * FINE] + early[:, q * FINE : (q + 1) * FINE]
        for x in range(4):
            for core in range(2):
                for e in range(2):
                    for h in range(2):
                        beams2[z, x, core, e * 8 : e * 8 + 8, h * FINE : (h + 1) * FINE] = beams[
                            h, pl.ds(x * 4 + core * 2 + e, 8, stride=16), :
                        ]

    def pack0(s, carry):
        bsend0[s] = beams2[s // 4, s % 4, 1 - my_core].astype(bf16)
        return carry

    lax.fori_loop(0, 32, pack0, 0)
    sibling = my_z * 8 + my_x * 2 + 1 - my_core
    core_copy = pltpu.make_async_remote_copy(
        src_ref=bsend0, dst_ref=brecv0, send_sem=bsend_sem.at[0], recv_sem=brecv_sem.at[0],
        **to({"af": sibling}),
    )
    core_copy.start()

    distribute(3)

    core_copy.wait()

    def pack1(s, carry):
        total = beams2[s // 4, s % 4, my_core] + brecv0[s].astype(f32)
        beams2[s // 4, s % 4, my_core] = total
        bsend1[s % 4, s // 4] = total.astype(bf16)
        return carry

    lax.fori_loop(0, 32, pack1, 0)
    x_copies = []
    for d in range(1, 4):
        x = (my_x + d) % 4
        x_copies.append(
            pltpu.make_async_remote_copy(
                src_ref=bsend1.at[x], dst_ref=brecv1.at[d - 1],
                send_sem=bsend_sem.at[d], recv_sem=brecv_sem.at[d],
                **to({"af": my_z * 8 + x * 2 + my_core}),
            )
        )
        x_copies[-1].start()

    distribute(4)

    for copy in x_copies:
        copy.wait()

    def pack2(zz, carry):
        total = beams2[zz, my_x, my_core]
        for d in range(3):
            total = total + brecv1[d, zz].astype(f32)
        beams2[zz, my_x, my_core] = total
        bsend2[zz] = total.astype(bf16)
        return carry

    lax.fori_loop(0, 8, pack2, 0)
    z_copies = []
    for d in range(1, 8):
        zz = (my_z + d) % 8
        z_copies.append(
            pltpu.make_async_remote_copy(
                src_ref=bsend2.at[zz], dst_ref=brecv2.at[d - 1],
                send_sem=bsend_sem.at[3 + d], recv_sem=brecv_sem.at[3 + d],
                **to({"af": zz * 8 + my_low}),
            )
        )
        z_copies[-1].start()

    def correlate(pair, fresh):
        turn_over(arrived.at[pair], turned, my_core)

        def keep(bi, bj, value):
            acc[bi, bj] = value if fresh else acc[bi, bj] + value

        products(arrived.at[pair], turned, keep)

    await_part(0)
    await_part(1)
    correlate(0, True)
    await_part(2)
    correlate(1, False)
    await_part(3)
    correlate(2, False)
    acc_copy = pltpu.make_async_copy(acc, acc_out, acc_sem)
    acc_copy.start()

    for copy in z_copies:
        copy.wait()
    total = beams2[my_z, my_x, my_core]
    for d in range(7):
        total = total + brecv2[d].astype(f32)
    beam_out[...] = total

    for step in range(STEPS):
        others = y_part(ysend, step, pl.ds(0, GROUPS - 1))
        pltpu.make_async_copy(others, others, ysend_sem.at[step]).wait()
        others = leaving(step, pl.ds(0, BINS - 1))
        pltpu.make_async_copy(others, others, send_sem.at[step]).wait()
    acc_copy.wait()
    pltpu.make_async_copy(outgo.at[PAIRS - 1, me], last.at[own_rows], own_sem).wait()
    await_part(STEPS - 1)


def turn_over(source, target, core):
    sign = jnp.where(iota((256, FINE), 1) < 64, 1.0, -1.0) * (1 - 2 * core).astype(jnp.float32)
    for bi in range(4):
        for t in range(2):
            rows, cols = slice(bi * 256, (bi + 1) * 256), slice(t * FINE, (t + 1) * FINE)
            swapped = pltpu.roll(source[rows, cols].astype(jnp.float32), 64, 1)
            target[rows, cols] = (swapped * sign).astype(jnp.bfloat16)


def products(plain, turned, keep):
    diagonal = iota((256, 256), 1) >= iota((256, 256), 0)
    for bi in range(4):
        rows = slice(bi * 256, (bi + 1) * 256)
        for bj in range(4):
            right = plain[bj * 256 : (bj + 1) * 256, :]
            if bj >= bi:
                real = lax.dot_general(plain[rows, :], right, CONTRACT_LANES, preferred_element_type=jnp.float32)
            if bj <= bi:
                imag = lax.dot_general(turned[rows, :], right, CONTRACT_LANES, preferred_element_type=jnp.float32)
            if bj > bi:
                value = real
            elif bj < bi:
                value = imag
            else:
                value = jnp.where(diagonal, real, imag)
            keep(bi, bj, value)


def finish(acc_in, last_in, beam_in, scale, vis, power, acc, last, turned, visbuf, acc_sem, last_sem, vis_sem):
    last_copy = pltpu.make_async_copy(last_in, last, last_sem)
    last_copy.start()
    acc_copies = [pltpu.make_async_copy(acc_in.at[b], acc.at[b], acc_sem.at[b]) for b in range(4)]
    for copy in acc_copies:
        copy.start()
    total = beam_in[...]
    square = total * total
    halves = [square[:, h * FINE : (h + 1) * FINE] for h in range(2)]
    halves = [half + pltpu.roll(half, 64, 1) for half in halves]
    for e in range(2):
        rows = slice(e * 8, (e + 1) * 8)
        by_time = jnp.concatenate([half[rows] for half in halves], axis=0).T
        for b in range(NB):
            power[b, e] = by_time[b * 8 : (b + 1) * 8, :]
    last_copy.wait()
    turn_over(last, turned, lax.axis_index("af") % 2)
    vis_copies = []

    def keep(bi, bj, value):
        if bj == 0:
            acc_copies[bi].wait()
        rows, cols = slice(bi * 256, (bi + 1) * 256), slice(bj * 256, (bj + 1) * 256)
        visbuf[rows, cols] = ((acc[bi, bj] + value) * scale[0:1, 0:1]).astype(jnp.bfloat16)
        if bj == 3:
            vis_copies.append(pltpu.make_async_copy(visbuf.at[rows], vis.at[rows], vis_sem.at[bi]))
            vis_copies[-1].start()

    products(last, turned, keep)
    for copy in vis_copies:
        copy.wait()


def per_device(volts, history, pfb_taps, zoom_bins, counts, beam_stations, beam_weights):
    vmem = pl.BlockSpec(memory_space=pltpu.VMEM)
    hbm = pl.BlockSpec(memory_space=pl.ANY)
    bf16, f32 = jnp.bfloat16, jnp.float32
    dma = pltpu.SemaphoreType.DMA
    acc, last, beam, scale = pl.pallas_call(
        kernel,
        out_shape=[
            jax.ShapeDtypeStruct((4, 4, 256, 256), f32),
            jax.ShapeDtypeStruct((NIN, LANES), bf16),
            jax.ShapeDtypeStruct((16, 2 * FINE), f32),
            jax.ShapeDtypeStruct((8, FINE), f32),
        ],
        in_specs=[hbm, hbm, vmem, vmem, vmem, vmem, vmem, vmem],
        out_specs=[hbm, hbm, vmem, vmem],
        scratch_shapes=[
            pltpu.VMEM((NT + TAPS - 1, COARSE, 2 * LOCAL, FINE), bf16),
            pltpu.VMEM((COARSE, 64, FINE), f32),
            pltpu.VMEM((PAIRS, GROUPS, 8, 16, FINE), bf16),
            pltpu.VMEM((PAIRS, GROUPS, 8, 16, FINE), bf16),
            pltpu.VMEM((CHG, FINE), bf16),
            pltpu.VMEM((8, CHG, 512), bf16),
            pltpu.VMEM((PAIRS, BINS, LOCAL, LANES), bf16),
            pltpu.VMEM((PAIRS - 1, NIN, LANES), bf16),
            pltpu.VMEM((NIN, LANES), bf16),
            pltpu.VMEM((4, 4, 256, 256), f32),
            pltpu.VMEM((16, FINE), f32),
            pltpu.VMEM((16, FINE), f32),
            pltpu.VMEM((2, FINE, FINE), f32),
            pltpu.VMEM((8, 4, 2, 16, 256), f32),
            pltpu.VMEM((32, 16, 256), bf16),
            pltpu.VMEM((32, 16, 256), bf16),
            pltpu.VMEM((4, 8, 16, 256), bf16),
            pltpu.VMEM((3, 8, 16, 256), bf16),
            pltpu.VMEM((8, 16, 256), bf16),
            pltpu.VMEM((7, 16, 256), bf16),
            dma((STEPS,)),
            dma((STEPS,)),
            dma((STEPS,)),
            dma((STEPS,)),
            dma((STEPS,)),
            dma((11,)),
            dma((11,)),
            dma,
            dma,
        ],
        compiler_params=pltpu.CompilerParams(
            collective_id=0, has_side_effects=True, vmem_limit_bytes=56 * 1024 * 1024
        ),
    )(
        volts, history, zoom_bins.reshape(FINE, FINE), counts.reshape(FINE, FINE),
        dft_rows(), pfb_taps, beam_stations, beam_weights.transpose(1, 0, 2),
    )
    vis, power = pl.pallas_call(
        finish,
        out_shape=[
            jax.ShapeDtypeStruct((NIN, NIN), bf16),
            jax.ShapeDtypeStruct((NB, 2, NT, COARSE), f32),
        ],
        in_specs=[hbm, hbm, vmem, vmem],
        out_specs=[hbm, vmem],
        scratch_shapes=[
            pltpu.VMEM((4, 4, 256, 256), f32),
            pltpu.VMEM((NIN, LANES), bf16),
            pltpu.VMEM((NIN, LANES), bf16),
            pltpu.VMEM((NIN, NIN), bf16),
            dma((4,)),
            dma,
            dma((4,)),
        ],
        compiler_params=pltpu.CompilerParams(vmem_limit_bytes=58 * 1024 * 1024),
    )(acc, last, beam, scale)
    return vis[None, None], power.transpose(0, 3, 1, 2)


def solution(mesh):
    in_specs = (P("af", "gx", None, None), P("af", "gx", None, None), P(), P(), P(), P(), P())
    out_specs = (P("af", "gx", None, None), P(None, "gx", "af", None))
    return jax.shard_map(
        per_device, mesh=mesh, in_specs=in_specs, out_specs=out_specs, check_vma=False
    )
```

time: 87.9 us -> 84.9 us (0.966)
  local copies, waits for them, and re-layouts: 6.48 us -> 0 us
  Pallas kernels: 80.4 us -> 83.9 us
    unnamed x2 -> x0, local copies, waits for them, and re-layouts: 4.53 us -> none
    pallas_call x1 -> x2, Pallas kernels: 80.4 us -> 83.9 us  [the longest x1 77.9 us: per_device(): pl.pallas_call(kernel, out_shape=[jax.ShapeDtypeStruct((4, 4, 256, 256),...]
    reshape x2 -> x0, local copies, waits for them, and re-layouts: 1.61 us -> none  [the longest x1 0.87 us: per_device(): split = power.reshape(2, 8, 2, 2, NT, 8)[:, :, :, 0, :, :NB]]
where the time goes in v3:
time: 84.9 us; the launch traced here: 84.7 us
  Pallas kernels  83.9 us (99%)
    pallas_call x1, Pallas kernels, per_device(): pl.pallas_call(kernel, out_shape=[jax.ShapeDtypeStruct((4, 4, 256, 256),...  77.9 us
    pallas_call x1, Pallas kernels, per_device(): pl.pallas_call(finish, out_shape=[jax.ShapeDtypeStruct((NIN, NIN), bf16),...  6 us

profile of v3, /device:TPU:1, one launch (start us, length us, event | category | flops | bytes accessed | tf_op | source)
XLA Modules:
  0.0 84.7 jit_solution(2275545913051959456)
XLA Ops:
  0.6 77.9 %shard_map.95 = (f32[4,4,256,256]{3,2,1,0:T(8,128)}, bf16[1024,256]{1,0:T(8,128)(2,1)}, f32[16,256]{1,0:T(8,128)}, f32[8,128]{1,0:T(8,128)}) custom-call(bf16[16,16,2,1024]{3,2,1,0:T(2,128)(2,1)} %volts.1, bf16[16,16,2,1408]{3,2,1,0:T(2,128)(2,1)} %history.1, s32[128,128]{1,0:T(8,128)} %bitcast.5, s32[128,128]{1,0:T(8,128)} %bitcast.6, ...), custom_call_target="tpu_custom_call" | custom-call | tf_op jit(solution)/shard_map/pallas_call | solution.py:495
  78.5 6.0 %shard_map.96 = (bf16[1024,1024]{1,0:T(8,128)(2,1)}, f32[6,2,8,16]{3,2,1,0:T(8,128)}) custom-call(f32[4,4,256,256]{3,2,1,0:T(8,128)} %get-tuple-element.8.acc_in, bf16[1024,256]{1,0:T(8,128)(2,1)} %get-tuple-element.9.last_in, f32[16,256]{1,0:T(8,128)} %get-tuple-element.10.beam_in, f32[8,128]{1,0:T(8,128)} %get-tuple-element.11.scale), custom_call_target="tpu_custom_call" | custom-call | tf_op jit(solution)/shard_map/pallas_call | solution.py:543
